TPU v7x, 128 devices: a whole 4x4x4 slice. The times are simulated.
128 devices in a mesh: dp: 8 (over z, x_lo), seq: 16 (over y, x_hi, core).
Axes of the slice: x: 4 (x_hi: 2, x_lo: 2; x = x_hi * 2 + x_lo), y: 4, z: 4, core: 2. Of those that a mesh axis runs over, the one named last changes fastest.
Arguments:
- frames: bfloat16 [8, 4096, 1536], P('dp', 'seq'), may hold values from -6 to 6
- upstream: bfloat16 [8, 4096, 1536], P('dp', 'seq'), may hold values from -6 to 6
- utt_span: int32 [2, 8, 4096], P(None, 'dp', 'seq'), may hold values from 0 to 4096, as said below
- w_qkv: bfloat16 [1536, 2304], P('dp')
- w_out: bfloat16 [768, 1536], P('dp'), may hold values from -0.21875 to 0.21875
Outputs:
- branch: bfloat16 [8, 4096, 1536], P('dp', 'seq')
- grad_in: bfloat16 [8, 4096, 1536], P('dp', 'seq')
- grad_qkv: float32 [1536, 2304], P(('dp', 'seq'))
- grad_out: float32 [768, 1536], P(('dp', 'seq'))
Inputs may be any that keep to these rules, and one draw needn't show every extreme that they name: In each row the utterances tile the frames: for frame i, utt_span[0] <= i < utt_span[1], and all frames of an utterance carry the same pair.
All inputs are finite; a program needn't handle non-finite values.
Results may differ from a plain program's by a relative error of at most 0.015.
Values may be sent and summed in bfloat16 or wider, within the bound.
No kernel may reach another device: no remote copies, remote signals or barrier semaphores. Data moves between devices by JAX's collectives and lax.ppermute only.
A program may use at most 128 MiB of HBM per device.

v0:
```python
import jax
import jax.numpy as jnp
from jax import lax
from jax.sharding import PartitionSpec as P

HEADS = 12
HEAD_DIM = 64
STRETCH = 64
PRIOR = 4
EPS = 1e-05


def from_behind(value, axis, by):
    length = lax.axis_size(axis)
    pairs = [(i, i + by) for i in range(length) if 0 <= i + by < length]
    return lax.ppermute(value, axis, pairs)


def normalize(inputs):
    widened = inputs.astype(jnp.float32)
    centered = widened - jnp.mean(widened, axis=-1, keepdims=True)
    inv_sigma = lax.rsqrt(jnp.mean(centered * centered, axis=-1, keepdims=True) + EPS)
    return (centered * inv_sigma, inv_sigma)


def contract(form, left, right):
    return jnp.einsum(form, left, right, preferred_element_type=jnp.float32)


def windows(extended):
    stretch_total = extended.shape[0] // STRETCH
    stretch_count = stretch_total - PRIOR
    blocked = extended.reshape((stretch_total, STRETCH) + extended.shape[1:])
    return jnp.concatenate(
        [blocked[shift_by : shift_by + stretch_count] for shift_by in range(PRIOR + 1)], axis=1
    )


def unwindow(windowed):
    stretch_count = windowed.shape[0]
    parted = windowed.reshape((stretch_count, PRIOR + 1, STRETCH) + windowed.shape[2:])
    running = jnp.zeros((stretch_count + PRIOR, STRETCH) + windowed.shape[2:], jnp.float32)
    for shift_by in range(PRIOR + 1):
        running = running.at[shift_by : shift_by + stretch_count].add(parted[:, shift_by])
    return running.reshape(((stretch_count + PRIOR) * STRETCH,) + windowed.shape[2:])


def visible(starts, limits, offset):
    stretch_count = starts.shape[0] // STRETCH
    block_first = jnp.arange(stretch_count, dtype=jnp.int32)[:, None] * STRETCH
    key_pos = (
        offset
        - PRIOR * STRETCH
        + block_first
        + jnp.arange((PRIOR + 1) * STRETCH, dtype=jnp.int32)[None, :]
    )
    lowest = starts.reshape(stretch_count, STRETCH)
    beyond = limits.reshape(stretch_count, STRETCH)
    return (key_pos[:, None, :] >= lowest[:, :, None]) & (key_pos[:, None, :] < beyond[:, :, None])


def attend_forward(queries, keys_ext, values_ext, mask):
    stretch_count = queries.shape[0] // STRETCH
    query_blocks = queries.reshape(stretch_count, STRETCH, HEADS, HEAD_DIM)
    key_windows = windows(keys_ext.reshape(-1, HEADS, HEAD_DIM))
    value_windows = windows(values_ext.reshape(-1, HEADS, HEAD_DIM))
    scores = contract("nqhd,nkhd->nhqk", query_blocks, key_windows) * HEAD_DIM ** (-0.5)
    allowed = mask[:, None]
    masked = jnp.where(allowed, scores, -1e30)
    highest = jnp.max(masked, axis=-1, keepdims=True)
    weights = jnp.where(allowed, jnp.exp(masked - highest), 0.0)
    probs = weights / jnp.sum(weights, axis=-1, keepdims=True)
    probs_low = probs.astype(jnp.bfloat16)
    context = contract("nhqk,nkhd->nqhd", probs_low, value_windows).astype(jnp.bfloat16)
    return (
        context.reshape(queries.shape),
        (query_blocks, key_windows, value_windows, probs, probs_low),
    )


def attend_backward(saved, d_context):
    query_blocks, key_windows, value_windows, probs, probs_low = saved
    d_blocks = d_context.reshape(query_blocks.shape)
    d_probs = contract("nqhd,nkhd->nhqk", d_blocks, value_windows)
    d_scores = probs * (d_probs - jnp.sum(probs * d_probs, axis=-1, keepdims=True))
    d_scores_low = (d_scores * HEAD_DIM ** (-0.5)).astype(jnp.bfloat16)
    d_queries = contract("nhqk,nkhd->nqhd", d_scores_low, key_windows).astype(jnp.bfloat16)
    d_keys = unwindow(contract("nhqk,nqhd->nkhd", d_scores_low, query_blocks))
    d_values = unwindow(contract("nhqk,nqhd->nkhd", probs_low, d_blocks))
    ext_rows = d_keys.shape[0]
    return (
        d_queries.reshape(d_context.shape),
        d_keys.reshape(ext_rows, -1),
        d_values.reshape(ext_rows, -1),
    )


def against_rows(left, piece_rows):
    return lax.dot_general(
        left, piece_rows, (((1,), (1,)), ((), ())), preferred_element_type=jnp.float32
    )


def over_frames(left, right):
    return lax.dot_general(
        left, right, (((0,), (0,)), ((), ())), preferred_element_type=jnp.float32
    )


def joint_term(left, right):
    return over_frames(left, right)


def body(frames, upstream, utt_span, w_qkv, w_out):
    own_frames = frames[0]
    own_grad = upstream[0]
    frame_count = own_frames.shape[0]
    inner_width = w_qkv.shape[1] // 3
    halo_rows = PRIOR * STRETCH
    offset = lax.axis_index("seq") * frame_count
    normed, inv_sigma = normalize(own_frames)
    normed_low = normed.astype(jnp.bfloat16)
    full_qkv, full_out = (
        lax.all_gather(w_qkv, "dp", axis=0, tiled=True),
        lax.all_gather(w_out, "dp", axis=0, tiled=True),
    )
    projected = jnp.dot(normed_low, full_qkv, preferred_element_type=jnp.float32)
    projected = projected.astype(jnp.bfloat16)
    queries = projected[:, :inner_width]
    keys_all = projected[:, inner_width : 2 * inner_width]
    values_all = projected[:, 2 * inner_width :]
    history = from_behind(jnp.stack([keys_all, values_all]), "seq", 1)
    keys_ext = jnp.concatenate([history[0], keys_all], axis=0)
    values_ext = jnp.concatenate([history[1], values_all], axis=0)
    context, saved = attend_forward(
        queries, keys_ext, values_ext, visible(utt_span[0, 0], utt_span[1, 0], offset)
    )
    branch = jnp.dot(context, full_out, preferred_element_type=jnp.float32)
    d_context = against_rows(own_grad, full_out)
    branch = branch.astype(jnp.bfloat16)
    d_context = d_context.astype(jnp.bfloat16)
    d_queries, d_keys, d_values = attend_backward(saved, d_context)
    returned = from_behind(
        jnp.stack([d_keys[:halo_rows], d_values[:halo_rows]]).astype(jnp.bfloat16), "seq", -1
    ).astype(jnp.float32)
    d_keys_own = (
        d_keys[halo_rows:].at[frame_count - halo_rows :].add(returned[0]).astype(jnp.bfloat16)
    )
    d_values_own = (
        d_values[halo_rows:].at[frame_count - halo_rows :].add(returned[1]).astype(jnp.bfloat16)
    )
    d_proj = jnp.concatenate([d_queries, d_keys_own, d_values_own], axis=1)
    grad_qkv = lax.psum_scatter(
        joint_term(normed_low, d_proj), ("dp", "seq"), scatter_dimension=0, tiled=True
    )
    grad_out = lax.psum_scatter(
        joint_term(context, own_grad), ("dp", "seq"), scatter_dimension=0, tiled=True
    )
    d_normed = against_rows(d_proj, full_qkv)
    grad_in = inv_sigma * (
        d_normed
        - jnp.mean(d_normed, axis=-1, keepdims=True)
        - normed * jnp.mean(d_normed * normed, axis=-1, keepdims=True)
    )
    return (branch[None], grad_in.astype(jnp.bfloat16)[None], grad_qkv, grad_out)


def solution(mesh):
    in_specs = (
        P("dp", "seq", None),
        P("dp", "seq", None),
        P(None, "dp", "seq"),
        P("dp", None),
        P("dp", None),
    )
    out_specs = (
        P("dp", "seq", None),
        P("dp", "seq", None),
        P(("dp", "seq"), None),
        P(("dp", "seq"), None),
    )
    return jax.shard_map(body, mesh=mesh, in_specs=in_specs, out_specs=out_specs, check_vma=False)
```

profile of v0, /device:TPU:8, one launch (start us, length us, event | category | flops | bytes accessed | tf_op | source)
XLA Modules:
  0.0 1096.6 jit_solution(9958152777341482748)
XLA Ops:
  11.1 144.9 %all-gather.3.cloned.1.call-done = bf16[1536,2304]{1,0:T(8,128)(2,1)} async-done(((bf16[192,2304]{1,0:T(8,128)(2,1)}), bf16[1536,2304]{1,0:T(8,128)(2,1)}) %all-gather.3.cloned.1.call-update) | async-done | bytes 7077904 | tf_op jit(solution)/shard_map/all_gather | solution.py:124
  156.0 5.1 convolution_convert_fusion
  164.6 58.0 %all-gather.5.cloned.1.call-done = bf16[768,1536]{1,0:T(8,128)(2,1)} async-done(((bf16[96,1536]{1,0:T(8,128)(2,1)}), bf16[768,1536]{1,0:T(8,128)(2,1)}) %all-gather.5.cloned.1.call-update) | async-done | bytes 2359312 | tf_op jit(solution)/shard_map/all_gather | solution.py:125
  257.2 4.6 concatenate.42
  261.8 4.2 fusion.87
  266.0 5.8 concatenate.44
  271.9 6.3 fusion.86
  278.1 4.4 fusion.51
  282.5 2.8 convolution_bitcast_fusion
  285.3 6.9 copy.108
  299.0 24.8 %fusion.20 = f32[4,320,12,64]{1,3,2,0:T(8,128)} fusion(bf16[4,64,12,64]{1,3,2,0:T(8,128)(2,1)S(1)} %copy-done.19, f32[4,12,64,320]{3,2,1,0:T(8,128)} %fusion.87, f32[4,12,64,320]{3,2,1,0:T(8,128)} %get-tuple-element.190, f32[4,12,64]{2,1,0:T(8,128)S(1)} %get-tuple-element.189), kind=kOutput, calls=%fused_computation.20 | convolution fusion | flops 132713792 | bytes 12201984 | tf_op jit(solution)/shard_map/nhqk,nqhd->nkhd/dot_general | solution.py:27
  324.9 6.9 copy.100
  341.1 4.3 collective-permute-start.1
  345.4 24.3 %fusion.52 = bf16[4,64,12,64]{1,3,2,0:T(8,128)(2,1)S(1)} fusion(bf16[4,320,12,64]{1,3,2,0:T(8,128)(2,1)} %concatenate.44, f32[4,12,64,320]{3,2,1,0:T(8,128)} %fusion.87, f32[4,12,64,320]{3,2,1,0:T(8,128)} %get-tuple-element.190, f32[4,12,64]{2,1,0:T(8,128)} %copy-done.78), kind=kOutput, calls=%fused_computation.63 | convolution fusion | flops 132910400 | bytes 10235904 | tf_op jit(solution)/shard_map/nhqk,nkhd->nqhd/dot_general | solution.py:27
  375.8 3.4 fusion.41
  382.8 3.0 fusion.62
  388.5 7.3 fusion.65
  395.8 379.2 %fusion.84 = (f32[16,2304]{1,0:T(8,128)S(1)}, f32[8,1536]{1,0:T(8,128)S(1)}) fusion(f32[1536,2304]{1,0:T(8,128)} %fusion.65, f32[768,1536]{1,0:T(8,128)} %fusion.62), kind=kCustom, calls=%all-reduce-scatter.2 | all-reduce-scatter fusion | flops 6291458 | bytes 19070976
  779.1 11.9 %collective-permute-start.62 = (f32[8,1536]{1,0:T(8,128)S(1)}, f32[8,1536]{1,0:T(8,128)S(1)}, u32[]{:S(2)}, u32[]{:S(2)}) collective-permute-start(f32[8,1536]{1,0:T(8,128)S(1)} %get-tuple-element.171), channel_id=1, source_target_pairs={{0,29},{1,30},{2,31},{3,32},{4,33},{5,34},{6,35},{7,36},{8,37},{9,... | collective-permute-start | bytes 147464
  799.2 15.5 %collective-permute-start.55 = (f32[8,1536]{1,0:T(8,128)S(1)}, f32[8,1536]{1,0:T(8,128)S(1)}, u32[]{:S(2)}, u32[]{:S(2)}) collective-permute-start(f32[8,1536]{1,0:T(8,128)S(1)} %get-tuple-element.171), channel_id=1, source_target_pairs={{0,22},{1,23},{2,24},{3,25},{4,26},{5,27},{6,28},{7,29},{8,30},{9,... | collective-permute-start | bytes 147464
  816.0 2.6 collective-permute-start.53
  818.6 2.9 collective-permute-start.52
  826.3 3.1 collective-permute-start.48
  831.9 3.5 collective-permute-start.46
  840.1 5.1 collective-permute-start.43
  848.9 5.8 collective-permute-start.40
  859.3 2.5 collective-permute-start.39
  863.8 2.8 collective-permute-start.37
  866.6 6.1 collective-permute-start.36
  872.7 3.1 collective-permute-start.35
  886.4 3.1 collective-permute-start.27
  889.5 3.3 fusion.14
  897.6 11.2 %collective-permute-done.29 = f32[16,2304]{1,0:T(8,128)S(1)} collective-permute-done((f32[16,2304]{1,0:T(8,128)S(1)}, f32[16,2304]{1,0:T(8,128)S(1)}, u32[]{:S(2)}, u32[]{:S(2)}) %collective-permute-start.29) | collective-permute-done | bytes 147488
  910.1 3.2 collective-permute-start.23
  915.5 5.3 fusion.83
  922.1 4.6 collective-permute-start.20
  932.4 4.3 collective-permute-start.16
  938.4 4.3 collective-permute-start.14
  942.8 5.7 collective-permute-start.13
  949.9 9.1 collective-permute-start.11
  960.9 5.9 collective-permute-start.9
  969.1 2.5 collective-permute-start.7
  973.1 28.8 %concatenate.47 = f32[262,1536]{1,0:T(8,128)S(1)} concatenate(f32[6,1536]{1,0:T(8,128)} %copy-done.49, f32[8,1536]{1,0:T(8,128)S(1)} %collective-permute-done.64, f32[8,1536]{1,0:T(8,128)} %copy-done.50, f32[8,1536]{1,0:T(8,128)} %copy-done.51, f32[8,1536]{1,0:T(8,128)} %copy-done.52, f32[8,1536]{1,0:T(8,128)} %copy-done.53, f32[8,1536]{1,0:T(8,128)} %copy-done.54, ...), dimensions={0} | concatenate | bytes 3219456
  1001.9 10.0 collective-permute-start.6
  1014.1 2.5 collective-permute-start.4
  1016.6 6.3 collective-permute-start.3
  1025.6 2.8 collective-permute-done.4
  1032.0 56.0 %concatenate.46 = f32[524,2304]{1,0:T(8,128)} concatenate(f32[12,2304]{1,0:T(8,128)} %collective-permute-done.33, f32[16,2304]{1,0:T(8,128)} %collective-permute-done.32, f32[16,2304]{1,0:T(8,128)S(1)} %copy-done.22, f32[16,2304]{1,0:T(8,128)S(1)} %copy-done.24, f32[16,2304]{1,0:T(8,128)S(1)} %copy-done.26, f32[16,2304]{1,0:T(8,128)S(1)} %collective-permute-done.28, ...), dimensions={0} | concatenate | bytes 9658368
  (341 shorter events, 150.2 us)
Async XLA Ops:
  7.2 148.8 %all-gather.3.cloned.1.call-start = ((), (), s32[]{:S(2)}) async-start(), calls=%async_computation | async-start | bytes 7962624 | tf_op jit(solution)/shard_map/all_gather | solution.py:124
  7.9 214.6 %all-gather.5.cloned.1.call-start = ((), (), s32[]{:S(2)}) async-start(), calls=%async_computation.1 | async-start | bytes 2654208 | tf_op jit(solution)/shard_map/all_gather | solution.py:125
  162.2 72.0 %collective-permute-start = (bf16[2,256,768]{2,1,0:T(8,128)(2,1)}, bf16[2,256,768]{2,1,0:T(8,128)(2,1)}, u32[]{:S(2)}, u32[]{:S(2)}) collective-permute-start(bf16[2,256,768]{2,1,0:T(8,128)(2,1)} %pad_maximum_fusion.1), channel_id=1, source_target_pairs={{0,1},{1,2},{2,3},{3,4},{4,5},{5,6},{6,7},{7,8},{8,9},{9,10},{10,1... | collective-permute-start | bytes 2359304 | tf_op jit(solution)/shard_map/ppermute | solution.py:16
  341.1 44.7 %collective-permute-start.1 = (bf16[2,256,768]{1,2,0:T(8,128)(2,1)}, bf16[2,256,768]{1,2,0:T(8,128)(2,1)}, u32[]{:S(2)}, u32[]{:S(2)}) collective-permute-start(bf16[2,256,768]{1,2,0:T(8,128)(2,1)} %pad_maximum_fusion.2), channel_id=1, source_target_pairs={{1,0},{2,1},{3,2},{4,3},{5,4},{6,5},{7,6},{8,7},{9,8},{10,9},{11,1... | collective-permute-start | bytes 2359304 | tf_op jit(solution)/shard_map/ppermute | solution.py:16
  775.0 18.8 %collective-permute-start.64 = (f32[8,1536]{1,0:T(8,128)S(1)}, f32[8,1536]{1,0:T(8,128)S(1)}, u32[]{:S(2)}, u32[]{:S(2)}) collective-permute-start(f32[8,1536]{1,0:T(8,128)S(1)} %get-tuple-element.171), channel_id=1, source_target_pairs={{0,31},{1,32},{2,33},{3,34},{4,35},{5,36},{6,37},{7,38},{8,39},{9,... | collective-permute-start | bytes 147464
  776.5 16.1 %collective-permute-start.65 = (f32[6,1536]{1,0:T(8,128)S(1)}, f32[6,1536]{1,0:T(8,128)S(1)}, u32[]{:S(2)}, u32[]{:S(2)}) collective-permute-start(f32[6,1536]{1,0:T(8,128)S(1)} %slice.520), channel_id=1, source_target_pairs={{0,32},{1,33},{2,34},{3,35},{4,36},{5,37},{6,38},{7,39},{8,40},{9,... | collective-permute-start | bytes 110600
  777.8 17.4 %collective-permute-start.63 = (f32[8,1536]{1,0:T(8,128)S(1)}, f32[8,1536]{1,0:T(8,128)S(1)}, u32[]{:S(2)}, u32[]{:S(2)}) collective-permute-start(f32[8,1536]{1,0:T(8,128)S(1)} %get-tuple-element.171), channel_id=1, source_target_pairs={{0,30},{1,31},{2,32},{3,33},{4,34},{5,35},{6,36},{7,37},{8,38},{9,... | collective-permute-start | bytes 147464
  779.1 17.4 %collective-permute-start.62 = (f32[8,1536]{1,0:T(8,128)S(1)}, f32[8,1536]{1,0:T(8,128)S(1)}, u32[]{:S(2)}, u32[]{:S(2)}) collective-permute-start(f32[8,1536]{1,0:T(8,128)S(1)} %get-tuple-element.171), channel_id=1, source_target_pairs={{0,29},{1,30},{2,31},{3,32},{4,33},{5,34},{6,35},{7,36},{8,37},{9,... | collective-permute-start | bytes 147464
  793.9 20.7 %collective-permute-start.59 = (f32[8,1536]{1,0:T(8,128)S(1)}, f32[8,1536]{1,0:T(8,128)S(1)}, u32[]{:S(2)}, u32[]{:S(2)}) collective-permute-start(f32[8,1536]{1,0:T(8,128)S(1)} %get-tuple-element.171), channel_id=1, source_target_pairs={{0,26},{1,27},{2,28},{3,29},{4,30},{5,31},{6,32},{7,33},{8,34},{9,... | collective-permute-start | bytes 147464
  795.2 20.7 %collective-permute-start.58 = (f32[8,1536]{1,0:T(8,128)S(1)}, f32[8,1536]{1,0:T(8,128)S(1)}, u32[]{:S(2)}, u32[]{:S(2)}) collective-permute-start(f32[8,1536]{1,0:T(8,128)S(1)} %get-tuple-element.171), channel_id=1, source_target_pairs={{0,25},{1,26},{2,27},{3,28},{4,29},{5,30},{6,31},{7,32},{8,33},{9,... | collective-permute-start | bytes 147464
  796.5 22.0 %collective-permute-start.57 = (f32[8,1536]{1,0:T(8,128)S(1)}, f32[8,1536]{1,0:T(8,128)S(1)}, u32[]{:S(2)}, u32[]{:S(2)}) collective-permute-start(f32[8,1536]{1,0:T(8,128)S(1)} %get-tuple-element.171), channel_id=1, source_target_pairs={{0,24},{1,25},{2,26},{3,27},{4,28},{5,29},{6,30},{7,31},{8,32},{9,... | collective-permute-start | bytes 147464
  797.8 23.6 %collective-permute-start.56 = (f32[8,1536]{1,0:T(8,128)S(1)}, f32[8,1536]{1,0:T(8,128)S(1)}, u32[]{:S(2)}, u32[]{:S(2)}) collective-permute-start(f32[8,1536]{1,0:T(8,128)S(1)} %get-tuple-element.171), channel_id=1, source_target_pairs={{0,23},{1,24},{2,25},{3,26},{4,27},{5,28},{6,29},{7,30},{8,31},{9,... | collective-permute-start | bytes 147464
  799.2 24.5 %collective-permute-start.55 = (f32[8,1536]{1,0:T(8,128)S(1)}, f32[8,1536]{1,0:T(8,128)S(1)}, u32[]{:S(2)}, u32[]{:S(2)}) collective-permute-start(f32[8,1536]{1,0:T(8,128)S(1)} %get-tuple-element.171), channel_id=1, source_target_pairs={{0,22},{1,23},{2,24},{3,25},{4,26},{5,27},{6,28},{7,29},{8,30},{9,... | collective-permute-start | bytes 147464
  826.3 13.8 %collective-permute-start.48 = (f32[8,1536]{1,0:T(8,128)S(1)}, f32[8,1536]{1,0:T(8,128)S(1)}, u32[]{:S(2)}, u32[]{:S(2)}) collective-permute-start(f32[8,1536]{1,0:T(8,128)S(1)} %get-tuple-element.171), channel_id=1, source_target_pairs={{0,15},{1,16},{2,17},{3,18},{4,19},{5,20},{6,21},{7,22},{8,23},{9,... | collective-permute-start | bytes 147464
  829.5 15.8 %collective-permute-start.47 = (f32[8,1536]{1,0:T(8,128)S(1)}, f32[8,1536]{1,0:T(8,128)S(1)}, u32[]{:S(2)}, u32[]{:S(2)}) collective-permute-start(f32[8,1536]{1,0:T(8,128)S(1)} %get-tuple-element.171), channel_id=1, source_target_pairs={{0,14},{1,15},{2,16},{3,17},{4,18},{5,19},{6,20},{7,21},{8,22},{9,... | collective-permute-start | bytes 147464
  831.9 14.7 %collective-permute-start.46 = (f32[8,1536]{1,0:T(8,128)S(1)}, f32[8,1536]{1,0:T(8,128)S(1)}, u32[]{:S(2)}, u32[]{:S(2)}) collective-permute-start(f32[8,1536]{1,0:T(8,128)S(1)} %get-tuple-element.171), channel_id=1, source_target_pairs={{0,13},{1,14},{2,15},{3,16},{4,17},{5,18},{6,19},{7,20},{8,21},{9,... | collective-permute-start | bytes 147464
  837.7 17.0 %collective-permute-start.44 = (f32[8,1536]{1,0:T(8,128)S(1)}, f32[8,1536]{1,0:T(8,128)S(1)}, u32[]{:S(2)}, u32[]{:S(2)}) collective-permute-start(f32[8,1536]{1,0:T(8,128)S(1)} %get-tuple-element.171), channel_id=1, source_target_pairs={{0,11},{1,12},{2,13},{3,14},{4,15},{5,16},{6,17},{7,18},{8,19},{9,... | collective-permute-start | bytes 147464
  840.1 17.1 %collective-permute-start.43 = (f32[8,1536]{1,0:T(8,128)S(1)}, f32[8,1536]{1,0:T(8,128)S(1)}, u32[]{:S(2)}, u32[]{:S(2)}) collective-permute-start(f32[8,1536]{1,0:T(8,128)S(1)} %get-tuple-element.171), channel_id=1, source_target_pairs={{0,10},{1,11},{2,12},{3,13},{4,14},{5,15},{6,16},{7,17},{8,18},{9,... | collective-permute-start | bytes 147464
  845.3 13.9 %collective-permute-start.42 = (f32[8,1536]{1,0:T(8,128)S(1)}, f32[8,1536]{1,0:T(8,128)S(1)}, u32[]{:S(2)}, u32[]{:S(2)}) collective-permute-start(f32[8,1536]{1,0:T(8,128)S(1)} %get-tuple-element.171), channel_id=1, source_target_pairs={{0,9},{1,10},{2,11},{3,12},{4,13},{5,14},{6,15},{7,16},{8,17},{9,1... | collective-permute-start | bytes 147464
  846.6 15.2 %collective-permute-start.41 = (f32[8,1536]{1,0:T(8,128)S(1)}, f32[8,1536]{1,0:T(8,128)S(1)}, u32[]{:S(2)}, u32[]{:S(2)}) collective-permute-start(f32[8,1536]{1,0:T(8,128)S(1)} %get-tuple-element.171), channel_id=1, source_target_pairs={{0,8},{1,9},{2,10},{3,11},{4,12},{5,13},{6,14},{7,15},{8,16},{9,17... | collective-permute-start | bytes 147464
  848.9 14.8 %collective-permute-start.40 = (f32[8,1536]{1,0:T(8,128)S(1)}, f32[8,1536]{1,0:T(8,128)S(1)}, u32[]{:S(2)}, u32[]{:S(2)}) collective-permute-start(f32[8,1536]{1,0:T(8,128)S(1)} %get-tuple-element.171), channel_id=1, source_target_pairs={{0,7},{1,8},{2,9},{3,10},{4,11},{5,12},{6,13},{7,14},{8,15},{9,16}... | collective-permute-start | bytes 147464
  855.3 31.1 %collective-permute-start.32 = (f32[16,2304]{1,0:T(8,128)S(1)}, f32[16,2304]{1,0:T(8,128)}, u32[]{:S(2)}, u32[]{:S(2)}) collective-permute-start(f32[16,2304]{1,0:T(8,128)S(1)} %get-tuple-element.170), channel_id=1, source_target_pairs={{0,31},{1,32},{2,33},{3,34},{4,35},{5,36},{6,37},{7,38},{8,39},{9,... | collective-permute-start | bytes 442376
  857.3 27.7 %collective-permute-start.33 = (f32[12,2304]{1,0:T(8,128)S(1)}, f32[12,2304]{1,0:T(8,128)}, u32[]{:S(2)}, u32[]{:S(2)}) collective-permute-start(f32[12,2304]{1,0:T(8,128)S(1)} %slice.519), channel_id=1, source_target_pairs={{0,32},{1,33},{2,34},{3,35},{4,36},{5,37},{6,38},{7,39},{8,40},{9,... | collective-permute-start | bytes 331784
  877.8 15.0 %collective-permute-start.31 = (f32[16,2304]{1,0:T(8,128)S(1)}, f32[16,2304]{1,0:T(8,128)S(1)}, u32[]{:S(2)}, u32[]{:S(2)}) collective-permute-start(f32[16,2304]{1,0:T(8,128)S(1)} %get-tuple-element.170), channel_id=1, source_target_pairs={{0,30},{1,31},{2,32},{3,33},{4,34},{5,35},{6,36},{7,37},{8,38},{9,... | collective-permute-start | bytes 442376
  881.2 15.1 %collective-permute-start.30 = (f32[16,2304]{1,0:T(8,128)S(1)}, f32[16,2304]{1,0:T(8,128)S(1)}, u32[]{:S(2)}, u32[]{:S(2)}) collective-permute-start(f32[16,2304]{1,0:T(8,128)S(1)} %get-tuple-element.170), channel_id=1, source_target_pairs={{0,29},{1,30},{2,31},{3,32},{4,33},{5,34},{6,35},{7,36},{8,37},{9,... | collective-permute-start | bytes 442376
  883.7 25.0 %collective-permute-start.29 = (f32[16,2304]{1,0:T(8,128)S(1)}, f32[16,2304]{1,0:T(8,128)S(1)}, u32[]{:S(2)}, u32[]{:S(2)}) collective-permute-start(f32[16,2304]{1,0:T(8,128)S(1)} %get-tuple-element.170), channel_id=1, source_target_pairs={{0,28},{1,29},{2,30},{3,31},{4,32},{5,33},{6,34},{7,35},{8,36},{9,... | collective-permute-start | bytes 442376
  885.0 25.0 %collective-permute-start.28 = (f32[16,2304]{1,0:T(8,128)S(1)}, f32[16,2304]{1,0:T(8,128)S(1)}, u32[]{:S(2)}, u32[]{:S(2)}) collective-permute-start(f32[16,2304]{1,0:T(8,128)S(1)} %get-tuple-element.170), channel_id=1, source_target_pairs={{0,27},{1,28},{2,29},{3,30},{4,31},{5,32},{6,33},{7,34},{8,35},{9,... | collective-permute-start | bytes 442376
  886.4 26.9 %collective-permute-start.27 = (f32[16,2304]{1,0:T(8,128)S(1)}, f32[16,2304]{1,0:T(8,128)S(1)}, u32[]{:S(2)}, u32[]{:S(2)}) collective-permute-start(f32[16,2304]{1,0:T(8,128)S(1)} %get-tuple-element.170), channel_id=1, source_target_pairs={{0,26},{1,27},{2,28},{3,29},{4,30},{5,31},{6,32},{7,33},{8,34},{9,... | collective-permute-start | bytes 442376
  892.9 27.9 %collective-permute-start.26 = (f32[16,2304]{1,0:T(8,128)S(1)}, f32[16,2304]{1,0:T(8,128)S(1)}, u32[]{:S(2)}, u32[]{:S(2)}) collective-permute-start(f32[16,2304]{1,0:T(8,128)S(1)} %get-tuple-element.170), channel_id=1, source_target_pairs={{0,25},{1,26},{2,27},{3,28},{4,29},{5,30},{6,31},{7,32},{8,33},{9,... | collective-permute-start | bytes 442376
  896.3 25.8 %collective-permute-start.25 = (f32[16,2304]{1,0:T(8,128)S(1)}, f32[16,2304]{1,0:T(8,128)S(1)}, u32[]{:S(2)}, u32[]{:S(2)}) collective-permute-start(f32[16,2304]{1,0:T(8,128)S(1)} %get-tuple-element.170), channel_id=1, source_target_pairs={{0,24},{1,25},{2,26},{3,27},{4,28},{5,29},{6,30},{7,31},{8,32},{9,... | collective-permute-start | bytes 442376
  908.8 17.9 %collective-permute-start.24 = (f32[16,2304]{1,0:T(8,128)S(1)}, f32[16,2304]{1,0:T(8,128)S(1)}, u32[]{:S(2)}, u32[]{:S(2)}) collective-permute-start(f32[16,2304]{1,0:T(8,128)S(1)} %get-tuple-element.170), channel_id=1, source_target_pairs={{0,23},{1,24},{2,25},{3,26},{4,27},{5,28},{6,29},{7,30},{8,31},{9,... | collective-permute-start | bytes 442376
  910.1 19.1 %collective-permute-start.23 = (f32[16,2304]{1,0:T(8,128)S(1)}, f32[16,2304]{1,0:T(8,128)S(1)}, u32[]{:S(2)}, u32[]{:S(2)}) collective-permute-start(f32[16,2304]{1,0:T(8,128)S(1)} %get-tuple-element.170), channel_id=1, source_target_pairs={{0,22},{1,23},{2,24},{3,25},{4,26},{5,27},{6,28},{7,29},{8,30},{9,... | collective-permute-start | bytes 442376
  914.0 16.6 %collective-permute-start.22 = (f32[16,2304]{1,0:T(8,128)S(1)}, f32[16,2304]{1,0:T(8,128)S(1)}, u32[]{:S(2)}, u32[]{:S(2)}) collective-permute-start(f32[16,2304]{1,0:T(8,128)S(1)} %get-tuple-element.170), channel_id=1, source_target_pairs={{0,21},{1,22},{2,23},{3,24},{4,25},{5,26},{6,27},{7,28},{8,29},{9,... | collective-permute-start | bytes 442376
  922.1 14.6 %collective-permute-start.20 = (f32[16,2304]{1,0:T(8,128)S(1)}, f32[16,2304]{1,0:T(8,128)S(1)}, u32[]{:S(2)}, u32[]{:S(2)}) collective-permute-start(f32[16,2304]{1,0:T(8,128)S(1)} %get-tuple-element.170), channel_id=1, source_target_pairs={{0,19},{1,20},{2,21},{3,22},{4,23},{5,24},{6,25},{7,26},{8,27},{9,... | collective-permute-start | bytes 442376
  930.5 18.0 %collective-permute-start.17 = (f32[16,2304]{1,0:T(8,128)S(1)}, f32[16,2304]{1,0:T(8,128)S(1)}, u32[]{:S(2)}, u32[]{:S(2)}) collective-permute-start(f32[16,2304]{1,0:T(8,128)S(1)} %get-tuple-element.170), channel_id=1, source_target_pairs={{0,16},{1,17},{2,18},{3,19},{4,20},{5,21},{6,22},{7,23},{8,24},{9,... | collective-permute-start | bytes 442376
  932.4 17.4 %collective-permute-start.16 = (f32[16,2304]{1,0:T(8,128)S(1)}, f32[16,2304]{1,0:T(8,128)S(1)}, u32[]{:S(2)}, u32[]{:S(2)}) collective-permute-start(f32[16,2304]{1,0:T(8,128)S(1)} %get-tuple-element.170), channel_id=1, source_target_pairs={{0,15},{1,16},{2,17},{3,18},{4,19},{5,20},{6,21},{7,22},{8,23},{9,... | collective-permute-start | bytes 442376
  936.7 22.2 %collective-permute-start.15 = (f32[16,2304]{1,0:T(8,128)S(1)}, f32[16,2304]{1,0:T(8,128)S(1)}, u32[]{:S(2)}, u32[]{:S(2)}) collective-permute-start(f32[16,2304]{1,0:T(8,128)S(1)} %get-tuple-element.170), channel_id=1, source_target_pairs={{0,14},{1,15},{2,16},{3,17},{4,18},{5,19},{6,20},{7,21},{8,22},{9,... | collective-permute-start | bytes 442376
  938.4 22.5 %collective-permute-start.14 = (f32[16,2304]{1,0:T(8,128)S(1)}, f32[16,2304]{1,0:T(8,128)S(1)}, u32[]{:S(2)}, u32[]{:S(2)}) collective-permute-start(f32[16,2304]{1,0:T(8,128)S(1)} %get-tuple-element.170), channel_id=1, source_target_pairs={{0,13},{1,14},{2,15},{3,16},{4,17},{5,18},{6,19},{7,20},{8,21},{9,... | collective-permute-start | bytes 442376
  942.8 24.0 %collective-permute-start.13 = (f32[16,2304]{1,0:T(8,128)S(1)}, f32[16,2304]{1,0:T(8,128)S(1)}, u32[]{:S(2)}, u32[]{:S(2)}) collective-permute-start(f32[16,2304]{1,0:T(8,128)S(1)} %get-tuple-element.170), channel_id=1, source_target_pairs={{0,12},{1,13},{2,14},{3,15},{4,16},{5,17},{6,18},{7,19},{8,20},{9,... | collective-permute-start | bytes 442376
  948.5 20.5 %collective-permute-start.12 = (f32[16,2304]{1,0:T(8,128)S(1)}, f32[16,2304]{1,0:T(8,128)S(1)}, u32[]{:S(2)}, u32[]{:S(2)}) collective-permute-start(f32[16,2304]{1,0:T(8,128)S(1)} %get-tuple-element.170), channel_id=1, source_target_pairs={{0,11},{1,12},{2,13},{3,14},{4,15},{5,16},{6,17},{7,18},{8,19},{9,... | collective-permute-start | bytes 442376
  949.9 52.0 %collective-permute-start.11 = (f32[16,2304]{1,0:T(8,128)S(1)}, f32[16,2304]{1,0:T(8,128)}, u32[]{:S(2)}, u32[]{:S(2)}) collective-permute-start(f32[16,2304]{1,0:T(8,128)S(1)} %get-tuple-element.170), channel_id=1, source_target_pairs={{0,10},{1,11},{2,12},{3,13},{4,14},{5,15},{6,16},{7,17},{8,18},{9,... | collective-permute-start | bytes 442376
  959.0 52.9 %collective-permute-start.10 = (f32[16,2304]{1,0:T(8,128)S(1)}, f32[16,2304]{1,0:T(8,128)}, u32[]{:S(2)}, u32[]{:S(2)}) collective-permute-start(f32[16,2304]{1,0:T(8,128)S(1)} %get-tuple-element.170), channel_id=1, source_target_pairs={{0,9},{1,10},{2,11},{3,12},{4,13},{5,14},{6,15},{7,16},{8,17},{9,1... | collective-permute-start | bytes 442376
  960.9 53.1 %collective-permute-start.9 = (f32[16,2304]{1,0:T(8,128)S(1)}, f32[16,2304]{1,0:T(8,128)}, u32[]{:S(2)}, u32[]{:S(2)}) collective-permute-start(f32[16,2304]{1,0:T(8,128)S(1)} %get-tuple-element.170), channel_id=1, source_target_pairs={{0,8},{1,9},{2,10},{3,11},{4,12},{5,13},{6,14},{7,15},{8,16},{9,17... | collective-permute-start | bytes 442376
  966.8 49.8 %collective-permute-start.8 = (f32[16,2304]{1,0:T(8,128)S(1)}, f32[16,2304]{1,0:T(8,128)}, u32[]{:S(2)}, u32[]{:S(2)}) collective-permute-start(f32[16,2304]{1,0:T(8,128)S(1)} %get-tuple-element.170), channel_id=1, source_target_pairs={{0,7},{1,8},{2,9},{3,10},{4,11},{5,12},{6,13},{7,14},{8,15},{9,16}... | collective-permute-start | bytes 442376
  969.1 53.9 %collective-permute-start.7 = (f32[16,2304]{1,0:T(8,128)S(1)}, f32[16,2304]{1,0:T(8,128)}, u32[]{:S(2)}, u32[]{:S(2)}) collective-permute-start(f32[16,2304]{1,0:T(8,128)S(1)} %get-tuple-element.170), channel_id=1, source_target_pairs={{0,6},{1,7},{2,8},{3,9},{4,10},{5,11},{6,12},{7,13},{8,14},{9,15},... | collective-permute-start | bytes 442376
  1001.9 23.6 %collective-permute-start.6 = (f32[16,2304]{1,0:T(8,128)S(1)}, f32[16,2304]{1,0:T(8,128)S(1)}, u32[]{:S(2)}, u32[]{:S(2)}) collective-permute-start(f32[16,2304]{1,0:T(8,128)S(1)} %get-tuple-element.170), channel_id=1, source_target_pairs={{0,5},{1,6},{2,7},{3,8},{4,9},{5,10},{6,11},{7,12},{8,13},{9,14},{... | collective-permute-start | bytes 442376
  1011.9 13.7 %collective-permute-start.5 = (f32[16,2304]{1,0:T(8,128)S(1)}, f32[16,2304]{1,0:T(8,128)S(1)}, u32[]{:S(2)}, u32[]{:S(2)}) collective-permute-start(f32[16,2304]{1,0:T(8,128)S(1)} %get-tuple-element.170), channel_id=1, source_target_pairs={{0,4},{1,5},{2,6},{3,7},{4,8},{5,9},{6,10},{7,11},{8,12},{9,13},{1... | collective-permute-start | bytes 442376
  1014.1 14.3 %collective-permute-start.4 = (f32[16,2304]{1,0:T(8,128)S(1)}, f32[16,2304]{1,0:T(8,128)S(1)}, u32[]{:S(2)}, u32[]{:S(2)}) collective-permute-start(f32[16,2304]{1,0:T(8,128)S(1)} %get-tuple-element.170), channel_id=1, source_target_pairs={{0,3},{1,4},{2,5},{3,6},{4,7},{5,8},{6,9},{7,10},{8,11},{9,12},{10... | collective-permute-start | bytes 442376
  (99 other events, 2466.0 us)
Sparse Core Ops, SparseCore 0:
  9.7 146.3 all-gather.2
  157.7 64.8 all-gather.4
where the time goes:
time: 1110 us; the launch traced here: 1100 us
  blocking collectives  379 us (34%)
  waiting for transfers between devices  226 us (20%)
  starting transfers between devices  198 us (18%)
  local copies, waits for them, and re-layouts  167 us (15%)
  matrix products  93.3 us (8%)
  other arithmetic  16.8 us (2%)
  between operations  16.3 us (1%)
    unnamed x1, blocking collectives  379 us
    unnamed x64, starting transfers between devices  191 us
    all_gather x1, waiting for transfers between devices, body(): lax.all_gather(w_qkv, 'dp', axis=0, tiled=True)  145 us
    unnamed x164, local copies, waits for them, and re-layouts  95.8 us
    dot_general x5, matrix products, contract(): return jnp.einsum(form, left, right, preferred_element_type=jnp.float32)  60.5 us
    all_gather x1, waiting for transfers between devices, body(): lax.all_gather(w_out, 'dp', axis=0, tiled=True)  58 us
    unnamed x66, waiting for transfers between devices  23.2 us
    slice x20, local copies, waits for them, and re-layouts, windows(): blocked[shift_by:shift_by + stretch_count]  22.7 us
  transfers between devices with their start and end apart: 68, of which 8 were waited for; matrix products, arithmetic and copies ran while one was open for 9% of the time, Pallas kernels for 0%

commit v1 on v0

--- a/solution.py
+++ b/solution.py
@@ -121,7 +121,9 @@
     normed, inv_sigma = normalize(own_frames)
     normed_low = normed.astype(jnp.bfloat16)
     full_qkv, full_out = (
-        lax.all_gather(w_qkv, "dp", axis=0, tiled=True),
+        jnp.concatenate(
+            lax.all_to_all(jnp.stack([w_qkv] * lax.axis_size("dp")), "dp", 0, 0), axis=0
+        ),
         lax.all_gather(w_out, "dp", axis=0, tiled=True),
     )
     projected = jnp.dot(normed_low, full_qkv, preferred_element_type=jnp.float32)

time: 1110 us -> 1050 us (0.946)
  waiting for transfers between devices: 226 us -> 148 us
  blocking collectives: 379 us -> 391 us
    all_gather x1 -> x0, waiting for transfers between devices: 145 us -> none  [body(): lax.all_gather(w_qkv, 'dp', axis=0, tiled=True)]
    all_to_all x0 -> x1, waiting for transfers between devices: none -> 123 us  [body(): lax.all_to_all(jnp.stack([w_qkv] * lax.axis_size('dp')), 'dp', 0, 0)]
    all_gather x1, waiting for transfers between devices: 58 us -> 0.02 us  [body(): lax.all_gather(w_out, 'dp', axis=0, tiled=True)]
    unnamed x1, blocking collectives: 379 us -> 391 us
    unnamed x66 -> x65, waiting for transfers between devices: 23.2 us -> 22.5 us
    unnamed x164 -> x166, local copies, waits for them, and re-layouts: 95.8 us -> 95.8 us
where the time goes in v1:
time: 1050 us; the launch traced here: 1040 us
  blocking collectives  391 us (37%)
  starting transfers between devices  205 us (20%)
  local copies, waits for them, and re-layouts  171 us (16%)
  waiting for transfers between devices  148 us (14%)
  matrix products  93.3 us (9%)
  between operations  16.4 us (2%)
  other arithmetic  15.7 us (1%)
    unnamed x1, blocking collectives  391 us
    unnamed x64, starting transfers between devices  192 us
    all_to_all x1, waiting for transfers between devices, body(): lax.all_to_all(jnp.stack([w_qkv] * lax.axis_size('dp')), 'dp', 0, 0)  123 us
    unnamed x166, local copies, waits for them, and re-layouts  95.8 us
    dot_general x5, matrix products, contract(): return jnp.einsum(form, left, right, preferred_element_type=jnp.float32)  60.5 us
    slice x20, local copies, waits for them, and re-layouts, windows(): blocked[shift_by:shift_by + stretch_count]  22.7 us
    unnamed x65, waiting for transfers between devices  22.5 us
  transfers between devices with their start and end apart: 68, of which 8 were waited for; matrix products, arithmetic and copies ran while one was open for 9% of the time, Pallas kernels for 0%

profile of v1, /device:TPU:8, one launch (start us, length us, event | category | flops | bytes accessed | tf_op | source)
XLA Modules:
  0.0 1040.2 jit_solution(12390899254085569163)
XLA Ops:
  7.2 4.6 stack.32
  11.8 6.4 all-to-all-start
  19.5 123.3 %all-to-all-done = bf16[8,192,2304]{2,1,0:T(8,128)(2,1)} async-done(((bf16[8,192,2304]{2,1,0:T(8,128)(2,1)}), bf16[8,192,2304]{2,1,0:T(8,128)(2,1)}, u32[]{:S(2)}, u32[]{:S(2)}) %all-to-all-start) | async-done | bytes 7077920 | tf_op jit(solution)/shard_map/all_to_all | solution.py:125
  142.8 5.1 convolution_convert_fusion
  188.0 4.6 concatenate.42
  192.6 4.2 fusion.94
  196.8 5.8 concatenate.44
  202.6 6.3 fusion.93
  208.9 4.4 fusion.53
  213.3 2.8 convolution_bitcast_fusion
  216.1 6.9 copy.108
  229.7 24.8 %fusion.20 = f32[4,320,12,64]{1,3,2,0:T(8,128)} fusion(bf16[4,64,12,64]{1,3,2,0:T(8,128)(2,1)S(1)} %copy-done.19, f32[4,12,64,320]{3,2,1,0:T(8,128)} %fusion.94, f32[4,12,64,320]{3,2,1,0:T(8,128)} %get-tuple-element.190, f32[4,12,64]{2,1,0:T(8,128)S(1)} %get-tuple-element.189), kind=kOutput, calls=%fused_computation.23 | convolution fusion | flops 132713792 | bytes 12201984 | tf_op jit(solution)/shard_map/nhqk,nqhd->nkhd/dot_general | solution.py:27
  255.6 6.9 copy.100
  271.9 4.2 collective-permute-start.1
  276.1 24.3 %fusion.54 = bf16[4,64,12,64]{1,3,2,0:T(8,128)(2,1)S(1)} fusion(bf16[4,320,12,64]{1,3,2,0:T(8,128)(2,1)} %concatenate.44, f32[4,12,64,320]{3,2,1,0:T(8,128)} %fusion.94, f32[4,12,64,320]{3,2,1,0:T(8,128)} %get-tuple-element.190, f32[4,12,64]{2,1,0:T(8,128)} %copy-done.79), kind=kOutput, calls=%fused_computation.66 | convolution fusion | flops 132910400 | bytes 10235904 | tf_op jit(solution)/shard_map/nhqk,nkhd->nqhd/dot_general | solution.py:27
  306.4 3.4 fusion.43
  313.4 3.0 fusion.68
  319.1 7.3 fusion.60
  326.4 391.4 %fusion.91 = (f32[16,2304]{1,0:T(8,128)S(1)}, f32[8,1536]{1,0:T(8,128)S(1)}) fusion(f32[1536,2304]{1,0:T(8,128)} %fusion.60, f32[768,1536]{1,0:T(8,128)} %fusion.68), kind=kCustom, calls=%all-reduce-scatter.2 | all-reduce-scatter fusion | flops 6291458 | bytes 19070976
  721.9 12.4 %collective-permute-start.62 = (f32[8,1536]{1,0:T(8,128)S(1)}, f32[8,1536]{1,0:T(8,128)S(1)}, u32[]{:S(2)}, u32[]{:S(2)}) collective-permute-start(f32[8,1536]{1,0:T(8,128)S(1)} %get-tuple-element.171), channel_id=1, source_target_pairs={{0,29},{1,30},{2,31},{3,32},{4,33},{5,34},{6,35},{7,36},{8,37},{9,... | collective-permute-start | bytes 147464
  742.5 15.7 %collective-permute-start.55 = (f32[8,1536]{1,0:T(8,128)S(1)}, f32[8,1536]{1,0:T(8,128)S(1)}, u32[]{:S(2)}, u32[]{:S(2)}) collective-permute-start(f32[8,1536]{1,0:T(8,128)S(1)} %get-tuple-element.171), channel_id=1, source_target_pairs={{0,22},{1,23},{2,24},{3,25},{4,26},{5,27},{6,28},{7,29},{8,30},{9,... | collective-permute-start | bytes 147464
  759.5 2.6 collective-permute-start.53
  762.1 2.9 collective-permute-start.52
  769.9 3.1 collective-permute-start.48
  775.5 3.5 collective-permute-start.46
  783.7 5.1 collective-permute-start.43
  792.5 5.8 collective-permute-start.40
  802.8 2.5 collective-permute-start.39
  807.3 2.8 collective-permute-start.37
  810.1 6.1 collective-permute-start.36
  816.2 3.1 collective-permute-start.35
  830.0 3.1 collective-permute-start.27
  833.1 3.3 fusion.14
  841.1 11.2 %collective-permute-done.29 = f32[16,2304]{1,0:T(8,128)S(1)} collective-permute-done((f32[16,2304]{1,0:T(8,128)S(1)}, f32[16,2304]{1,0:T(8,128)S(1)}, u32[]{:S(2)}, u32[]{:S(2)}) %collective-permute-start.29) | collective-permute-done | bytes 147488
  853.6 3.2 collective-permute-start.23
  859.0 5.3 fusion.90
  865.7 4.6 collective-permute-start.20
  876.0 4.3 collective-permute-start.16
  882.0 4.3 collective-permute-start.14
  886.3 5.7 collective-permute-start.13
  893.4 9.1 collective-permute-start.11
  904.5 5.9 collective-permute-start.9
  916.6 28.8 %concatenate.47 = f32[262,1536]{1,0:T(8,128)S(1)} concatenate(f32[6,1536]{1,0:T(8,128)} %copy-done.49, f32[8,1536]{1,0:T(8,128)S(1)} %collective-permute-done.64, f32[8,1536]{1,0:T(8,128)} %copy-done.50, f32[8,1536]{1,0:T(8,128)} %copy-done.51, f32[8,1536]{1,0:T(8,128)} %copy-done.52, f32[8,1536]{1,0:T(8,128)} %copy-done.53, f32[8,1536]{1,0:T(8,128)} %copy-done.54, ...), dimensions={0} | concatenate | bytes 3219456
  945.5 10.0 collective-permute-start.6
  957.7 2.5 collective-permute-start.4
  960.2 6.3 collective-permute-start.3
  969.1 2.8 collective-permute-done.4
  975.6 56.0 %concatenate.46 = f32[524,2304]{1,0:T(8,128)} concatenate(f32[12,2304]{1,0:T(8,128)} %collective-permute-done.33, f32[16,2304]{1,0:T(8,128)} %collective-permute-done.32, f32[16,2304]{1,0:T(8,128)S(1)} %copy-done.22, f32[16,2304]{1,0:T(8,128)S(1)} %copy-done.24, f32[16,2304]{1,0:T(8,128)S(1)} %copy-done.26, f32[16,2304]{1,0:T(8,128)S(1)} %collective-permute-done.28, ...), dimensions={0} | concatenate | bytes 9658368
  (343 shorter events, 152.2 us)
Async XLA Ops:
  11.8 131.0 %all-to-all-start = ((bf16[8,192,2304]{2,1,0:T(8,128)(2,1)}), bf16[8,192,2304]{2,1,0:T(8,128)(2,1)}, u32[]{:S(2)}, u32[]{:S(2)}) async-start(bf16[8,192,2304]{2,1,0:T(8,128)(2,1)} %stack.32), calls=%async_computation | async-start | bytes 14155776 | tf_op jit(solution)/shard_map/all_to_all | solution.py:125
  18.1 133.2 %all-gather.2.cloned.1.call-start = ((), (), s32[]{:S(2)}) async-start(), calls=%async_computation.1 | async-start | bytes 2654208 | tf_op jit(solution)/shard_map/all_gather | solution.py:127
  149.0 16.0 %collective-permute-start = (bf16[2,256,768]{2,1,0:T(8,128)(2,1)}, bf16[2,256,768]{2,1,0:T(8,128)(2,1)}, u32[]{:S(2)}, u32[]{:S(2)}) collective-permute-start(bf16[2,256,768]{2,1,0:T(8,128)(2,1)} %pad_maximum_fusion.1), channel_id=1, source_target_pairs={{0,1},{1,2},{2,3},{3,4},{4,5},{5,6},{6,7},{7,8},{8,9},{9,10},{10,1... | collective-permute-start | bytes 2359304 | tf_op jit(solution)/shard_map/ppermute | solution.py:16
  271.9 44.5 %collective-permute-start.1 = (bf16[2,256,768]{1,2,0:T(8,128)(2,1)}, bf16[2,256,768]{1,2,0:T(8,128)(2,1)}, u32[]{:S(2)}, u32[]{:S(2)}) collective-permute-start(bf16[2,256,768]{1,2,0:T(8,128)(2,1)} %pad_maximum_fusion.2), channel_id=1, source_target_pairs={{1,0},{2,1},{3,2},{4,3},{5,4},{6,5},{7,6},{8,7},{9,8},{10,9},{11,1... | collective-permute-start | bytes 2359304 | tf_op jit(solution)/shard_map/ppermute | solution.py:16
  717.9 19.3 %collective-permute-start.64 = (f32[8,1536]{1,0:T(8,128)S(1)}, f32[8,1536]{1,0:T(8,128)S(1)}, u32[]{:S(2)}, u32[]{:S(2)}) collective-permute-start(f32[8,1536]{1,0:T(8,128)S(1)} %get-tuple-element.171), channel_id=1, source_target_pairs={{0,31},{1,32},{2,33},{3,34},{4,35},{5,36},{6,37},{7,38},{8,39},{9,... | collective-permute-start | bytes 147464
  719.3 16.6 %collective-permute-start.65 = (f32[6,1536]{1,0:T(8,128)S(1)}, f32[6,1536]{1,0:T(8,128)S(1)}, u32[]{:S(2)}, u32[]{:S(2)}) collective-permute-start(f32[6,1536]{1,0:T(8,128)S(1)} %slice.520), channel_id=1, source_target_pairs={{0,32},{1,33},{2,34},{3,35},{4,36},{5,37},{6,38},{7,39},{8,40},{9,... | collective-permute-start | bytes 110600
  720.6 17.9 %collective-permute-start.63 = (f32[8,1536]{1,0:T(8,128)S(1)}, f32[8,1536]{1,0:T(8,128)S(1)}, u32[]{:S(2)}, u32[]{:S(2)}) collective-permute-start(f32[8,1536]{1,0:T(8,128)S(1)} %get-tuple-element.171), channel_id=1, source_target_pairs={{0,30},{1,31},{2,32},{3,33},{4,34},{5,35},{6,36},{7,37},{8,38},{9,... | collective-permute-start | bytes 147464
  721.9 17.9 %collective-permute-start.62 = (f32[8,1536]{1,0:T(8,128)S(1)}, f32[8,1536]{1,0:T(8,128)S(1)}, u32[]{:S(2)}, u32[]{:S(2)}) collective-permute-start(f32[8,1536]{1,0:T(8,128)S(1)} %get-tuple-element.171), channel_id=1, source_target_pairs={{0,29},{1,30},{2,31},{3,32},{4,33},{5,34},{6,35},{7,36},{8,37},{9,... | collective-permute-start | bytes 147464
  737.2 21.0 %collective-permute-start.59 = (f32[8,1536]{1,0:T(8,128)S(1)}, f32[8,1536]{1,0:T(8,128)S(1)}, u32[]{:S(2)}, u32[]{:S(2)}) collective-permute-start(f32[8,1536]{1,0:T(8,128)S(1)} %get-tuple-element.171), channel_id=1, source_target_pairs={{0,26},{1,27},{2,28},{3,29},{4,30},{5,31},{6,32},{7,33},{8,34},{9,... | collective-permute-start | bytes 147464
  738.6 21.0 %collective-permute-start.58 = (f32[8,1536]{1,0:T(8,128)S(1)}, f32[8,1536]{1,0:T(8,128)S(1)}, u32[]{:S(2)}, u32[]{:S(2)}) collective-permute-start(f32[8,1536]{1,0:T(8,128)S(1)} %get-tuple-element.171), channel_id=1, source_target_pairs={{0,25},{1,26},{2,27},{3,28},{4,29},{5,30},{6,31},{7,32},{8,33},{9,... | collective-permute-start | bytes 147464
  739.9 22.2 %collective-permute-start.57 = (f32[8,1536]{1,0:T(8,128)S(1)}, f32[8,1536]{1,0:T(8,128)S(1)}, u32[]{:S(2)}, u32[]{:S(2)}) collective-permute-start(f32[8,1536]{1,0:T(8,128)S(1)} %get-tuple-element.171), channel_id=1, source_target_pairs={{0,24},{1,25},{2,26},{3,27},{4,28},{5,29},{6,30},{7,31},{8,32},{9,... | collective-permute-start | bytes 147464
  741.2 23.8 %collective-permute-start.56 = (f32[8,1536]{1,0:T(8,128)S(1)}, f32[8,1536]{1,0:T(8,128)S(1)}, u32[]{:S(2)}, u32[]{:S(2)}) collective-permute-start(f32[8,1536]{1,0:T(8,128)S(1)} %get-tuple-element.171), channel_id=1, source_target_pairs={{0,23},{1,24},{2,25},{3,26},{4,27},{5,28},{6,29},{7,30},{8,31},{9,... | collective-permute-start | bytes 147464
  742.5 24.7 %collective-permute-start.55 = (f32[8,1536]{1,0:T(8,128)S(1)}, f32[8,1536]{1,0:T(8,128)S(1)}, u32[]{:S(2)}, u32[]{:S(2)}) collective-permute-start(f32[8,1536]{1,0:T(8,128)S(1)} %get-tuple-element.171), channel_id=1, source_target_pairs={{0,22},{1,23},{2,24},{3,25},{4,26},{5,27},{6,28},{7,29},{8,30},{9,... | collective-permute-start | bytes 147464
  769.9 13.8 %collective-permute-start.48 = (f32[8,1536]{1,0:T(8,128)S(1)}, f32[8,1536]{1,0:T(8,128)S(1)}, u32[]{:S(2)}, u32[]{:S(2)}) collective-permute-start(f32[8,1536]{1,0:T(8,128)S(1)} %get-tuple-element.171), channel_id=1, source_target_pairs={{0,15},{1,16},{2,17},{3,18},{4,19},{5,20},{6,21},{7,22},{8,23},{9,... | collective-permute-start | bytes 147464
  773.0 15.8 %collective-permute-start.47 = (f32[8,1536]{1,0:T(8,128)S(1)}, f32[8,1536]{1,0:T(8,128)S(1)}, u32[]{:S(2)}, u32[]{:S(2)}) collective-permute-start(f32[8,1536]{1,0:T(8,128)S(1)} %get-tuple-element.171), channel_id=1, source_target_pairs={{0,14},{1,15},{2,16},{3,17},{4,18},{5,19},{6,20},{7,21},{8,22},{9,... | collective-permute-start | bytes 147464
  775.5 14.7 %collective-permute-start.46 = (f32[8,1536]{1,0:T(8,128)S(1)}, f32[8,1536]{1,0:T(8,128)S(1)}, u32[]{:S(2)}, u32[]{:S(2)}) collective-permute-start(f32[8,1536]{1,0:T(8,128)S(1)} %get-tuple-element.171), channel_id=1, source_target_pairs={{0,13},{1,14},{2,15},{3,16},{4,17},{5,18},{6,19},{7,20},{8,21},{9,... | collective-permute-start | bytes 147464
  781.2 17.0 %collective-permute-start.44 = (f32[8,1536]{1,0:T(8,128)S(1)}, f32[8,1536]{1,0:T(8,128)S(1)}, u32[]{:S(2)}, u32[]{:S(2)}) collective-permute-start(f32[8,1536]{1,0:T(8,128)S(1)} %get-tuple-element.171), channel_id=1, source_target_pairs={{0,11},{1,12},{2,13},{3,14},{4,15},{5,16},{6,17},{7,18},{8,19},{9,... | collective-permute-start | bytes 147464
  783.7 17.1 %collective-permute-start.43 = (f32[8,1536]{1,0:T(8,128)S(1)}, f32[8,1536]{1,0:T(8,128)S(1)}, u32[]{:S(2)}, u32[]{:S(2)}) collective-permute-start(f32[8,1536]{1,0:T(8,128)S(1)} %get-tuple-element.171), channel_id=1, source_target_pairs={{0,10},{1,11},{2,12},{3,13},{4,14},{5,15},{6,16},{7,17},{8,18},{9,... | collective-permute-start | bytes 147464
  788.9 13.9 %collective-permute-start.42 = (f32[8,1536]{1,0:T(8,128)S(1)}, f32[8,1536]{1,0:T(8,128)S(1)}, u32[]{:S(2)}, u32[]{:S(2)}) collective-permute-start(f32[8,1536]{1,0:T(8,128)S(1)} %get-tuple-element.171), channel_id=1, source_target_pairs={{0,9},{1,10},{2,11},{3,12},{4,13},{5,14},{6,15},{7,16},{8,17},{9,1... | collective-permute-start | bytes 147464
  790.2 15.2 %collective-permute-start.41 = (f32[8,1536]{1,0:T(8,128)S(1)}, f32[8,1536]{1,0:T(8,128)S(1)}, u32[]{:S(2)}, u32[]{:S(2)}) collective-permute-start(f32[8,1536]{1,0:T(8,128)S(1)} %get-tuple-element.171), channel_id=1, source_target_pairs={{0,8},{1,9},{2,10},{3,11},{4,12},{5,13},{6,14},{7,15},{8,16},{9,17... | collective-permute-start | bytes 147464
  792.5 14.8 %collective-permute-start.40 = (f32[8,1536]{1,0:T(8,128)S(1)}, f32[8,1536]{1,0:T(8,128)S(1)}, u32[]{:S(2)}, u32[]{:S(2)}) collective-permute-start(f32[8,1536]{1,0:T(8,128)S(1)} %get-tuple-element.171), channel_id=1, source_target_pairs={{0,7},{1,8},{2,9},{3,10},{4,11},{5,12},{6,13},{7,14},{8,15},{9,16}... | collective-permute-start | bytes 147464
  798.9 31.1 %collective-permute-start.32 = (f32[16,2304]{1,0:T(8,128)S(1)}, f32[16,2304]{1,0:T(8,128)}, u32[]{:S(2)}, u32[]{:S(2)}) collective-permute-start(f32[16,2304]{1,0:T(8,128)S(1)} %get-tuple-element.170), channel_id=1, source_target_pairs={{0,31},{1,32},{2,33},{3,34},{4,35},{5,36},{6,37},{7,38},{8,39},{9,... | collective-permute-start | bytes 442376
  800.9 27.7 %collective-permute-start.33 = (f32[12,2304]{1,0:T(8,128)S(1)}, f32[12,2304]{1,0:T(8,128)}, u32[]{:S(2)}, u32[]{:S(2)}) collective-permute-start(f32[12,2304]{1,0:T(8,128)S(1)} %slice.519), channel_id=1, source_target_pairs={{0,32},{1,33},{2,34},{3,35},{4,36},{5,37},{6,38},{7,39},{8,40},{9,... | collective-permute-start | bytes 331784
  821.4 15.0 %collective-permute-start.31 = (f32[16,2304]{1,0:T(8,128)S(1)}, f32[16,2304]{1,0:T(8,128)S(1)}, u32[]{:S(2)}, u32[]{:S(2)}) collective-permute-start(f32[16,2304]{1,0:T(8,128)S(1)} %get-tuple-element.170), channel_id=1, source_target_pairs={{0,30},{1,31},{2,32},{3,33},{4,34},{5,35},{6,36},{7,37},{8,38},{9,... | collective-permute-start | bytes 442376
  824.7 15.1 %collective-permute-start.30 = (f32[16,2304]{1,0:T(8,128)S(1)}, f32[16,2304]{1,0:T(8,128)S(1)}, u32[]{:S(2)}, u32[]{:S(2)}) collective-permute-start(f32[16,2304]{1,0:T(8,128)S(1)} %get-tuple-element.170), channel_id=1, source_target_pairs={{0,29},{1,30},{2,31},{3,32},{4,33},{5,34},{6,35},{7,36},{8,37},{9,... | collective-permute-start | bytes 442376
  827.3 25.0 %collective-permute-start.29 = (f32[16,2304]{1,0:T(8,128)S(1)}, f32[16,2304]{1,0:T(8,128)S(1)}, u32[]{:S(2)}, u32[]{:S(2)}) collective-permute-start(f32[16,2304]{1,0:T(8,128)S(1)} %get-tuple-element.170), channel_id=1, source_target_pairs={{0,28},{1,29},{2,30},{3,31},{4,32},{5,33},{6,34},{7,35},{8,36},{9,... | collective-permute-start | bytes 442376
  828.6 25.0 %collective-permute-start.28 = (f32[16,2304]{1,0:T(8,128)S(1)}, f32[16,2304]{1,0:T(8,128)S(1)}, u32[]{:S(2)}, u32[]{:S(2)}) collective-permute-start(f32[16,2304]{1,0:T(8,128)S(1)} %get-tuple-element.170), channel_id=1, source_target_pairs={{0,27},{1,28},{2,29},{3,30},{4,31},{5,32},{6,33},{7,34},{8,35},{9,... | collective-permute-start | bytes 442376
  830.0 26.9 %collective-permute-start.27 = (f32[16,2304]{1,0:T(8,128)S(1)}, f32[16,2304]{1,0:T(8,128)S(1)}, u32[]{:S(2)}, u32[]{:S(2)}) collective-permute-start(f32[16,2304]{1,0:T(8,128)S(1)} %get-tuple-element.170), channel_id=1, source_target_pairs={{0,26},{1,27},{2,28},{3,29},{4,30},{5,31},{6,32},{7,33},{8,34},{9,... | collective-permute-start | bytes 442376
  836.4 27.9 %collective-permute-start.26 = (f32[16,2304]{1,0:T(8,128)S(1)}, f32[16,2304]{1,0:T(8,128)S(1)}, u32[]{:S(2)}, u32[]{:S(2)}) collective-permute-start(f32[16,2304]{1,0:T(8,128)S(1)} %get-tuple-element.170), channel_id=1, source_target_pairs={{0,25},{1,26},{2,27},{3,28},{4,29},{5,30},{6,31},{7,32},{8,33},{9,... | collective-permute-start | bytes 442376
  839.8 25.8 %collective-permute-start.25 = (f32[16,2304]{1,0:T(8,128)S(1)}, f32[16,2304]{1,0:T(8,128)S(1)}, u32[]{:S(2)}, u32[]{:S(2)}) collective-permute-start(f32[16,2304]{1,0:T(8,128)S(1)} %get-tuple-element.170), channel_id=1, source_target_pairs={{0,24},{1,25},{2,26},{3,27},{4,28},{5,29},{6,30},{7,31},{8,32},{9,... | collective-permute-start | bytes 442376
  852.3 17.9 %collective-permute-start.24 = (f32[16,2304]{1,0:T(8,128)S(1)}, f32[16,2304]{1,0:T(8,128)S(1)}, u32[]{:S(2)}, u32[]{:S(2)}) collective-permute-start(f32[16,2304]{1,0:T(8,128)S(1)} %get-tuple-element.170), channel_id=1, source_target_pairs={{0,23},{1,24},{2,25},{3,26},{4,27},{5,28},{6,29},{7,30},{8,31},{9,... | collective-permute-start | bytes 442376
  853.6 19.1 %collective-permute-start.23 = (f32[16,2304]{1,0:T(8,128)S(1)}, f32[16,2304]{1,0:T(8,128)S(1)}, u32[]{:S(2)}, u32[]{:S(2)}) collective-permute-start(f32[16,2304]{1,0:T(8,128)S(1)} %get-tuple-element.170), channel_id=1, source_target_pairs={{0,22},{1,23},{2,24},{3,25},{4,26},{5,27},{6,28},{7,29},{8,30},{9,... | collective-permute-start | bytes 442376
  857.5 16.6 %collective-permute-start.22 = (f32[16,2304]{1,0:T(8,128)S(1)}, f32[16,2304]{1,0:T(8,128)S(1)}, u32[]{:S(2)}, u32[]{:S(2)}) collective-permute-start(f32[16,2304]{1,0:T(8,128)S(1)} %get-tuple-element.170), channel_id=1, source_target_pairs={{0,21},{1,22},{2,23},{3,24},{4,25},{5,26},{6,27},{7,28},{8,29},{9,... | collective-permute-start | bytes 442376
  865.7 14.6 %collective-permute-start.20 = (f32[16,2304]{1,0:T(8,128)S(1)}, f32[16,2304]{1,0:T(8,128)S(1)}, u32[]{:S(2)}, u32[]{:S(2)}) collective-permute-start(f32[16,2304]{1,0:T(8,128)S(1)} %get-tuple-element.170), channel_id=1, source_target_pairs={{0,19},{1,20},{2,21},{3,22},{4,23},{5,24},{6,25},{7,26},{8,27},{9,... | collective-permute-start | bytes 442376
  874.1 18.0 %collective-permute-start.17 = (f32[16,2304]{1,0:T(8,128)S(1)}, f32[16,2304]{1,0:T(8,128)S(1)}, u32[]{:S(2)}, u32[]{:S(2)}) collective-permute-start(f32[16,2304]{1,0:T(8,128)S(1)} %get-tuple-element.170), channel_id=1, source_target_pairs={{0,16},{1,17},{2,18},{3,19},{4,20},{5,21},{6,22},{7,23},{8,24},{9,... | collective-permute-start | bytes 442376
  876.0 17.4 %collective-permute-start.16 = (f32[16,2304]{1,0:T(8,128)S(1)}, f32[16,2304]{1,0:T(8,128)S(1)}, u32[]{:S(2)}, u32[]{:S(2)}) collective-permute-start(f32[16,2304]{1,0:T(8,128)S(1)} %get-tuple-element.170), channel_id=1, source_target_pairs={{0,15},{1,16},{2,17},{3,18},{4,19},{5,20},{6,21},{7,22},{8,23},{9,... | collective-permute-start | bytes 442376
  880.3 22.2 %collective-permute-start.15 = (f32[16,2304]{1,0:T(8,128)S(1)}, f32[16,2304]{1,0:T(8,128)S(1)}, u32[]{:S(2)}, u32[]{:S(2)}) collective-permute-start(f32[16,2304]{1,0:T(8,128)S(1)} %get-tuple-element.170), channel_id=1, source_target_pairs={{0,14},{1,15},{2,16},{3,17},{4,18},{5,19},{6,20},{7,21},{8,22},{9,... | collective-permute-start | bytes 442376
  882.0 22.4 %collective-permute-start.14 = (f32[16,2304]{1,0:T(8,128)S(1)}, f32[16,2304]{1,0:T(8,128)S(1)}, u32[]{:S(2)}, u32[]{:S(2)}) collective-permute-start(f32[16,2304]{1,0:T(8,128)S(1)} %get-tuple-element.170), channel_id=1, source_target_pairs={{0,13},{1,14},{2,15},{3,16},{4,17},{5,18},{6,19},{7,20},{8,21},{9,... | collective-permute-start | bytes 442376
  886.3 24.0 %collective-permute-start.13 = (f32[16,2304]{1,0:T(8,128)S(1)}, f32[16,2304]{1,0:T(8,128)S(1)}, u32[]{:S(2)}, u32[]{:S(2)}) collective-permute-start(f32[16,2304]{1,0:T(8,128)S(1)} %get-tuple-element.170), channel_id=1, source_target_pairs={{0,12},{1,13},{2,14},{3,15},{4,16},{5,17},{6,18},{7,19},{8,20},{9,... | collective-permute-start | bytes 442376
  892.1 20.5 %collective-permute-start.12 = (f32[16,2304]{1,0:T(8,128)S(1)}, f32[16,2304]{1,0:T(8,128)S(1)}, u32[]{:S(2)}, u32[]{:S(2)}) collective-permute-start(f32[16,2304]{1,0:T(8,128)S(1)} %get-tuple-element.170), channel_id=1, source_target_pairs={{0,11},{1,12},{2,13},{3,14},{4,15},{5,16},{6,17},{7,18},{8,19},{9,... | collective-permute-start | bytes 442376
  893.4 52.0 %collective-permute-start.11 = (f32[16,2304]{1,0:T(8,128)S(1)}, f32[16,2304]{1,0:T(8,128)}, u32[]{:S(2)}, u32[]{:S(2)}) collective-permute-start(f32[16,2304]{1,0:T(8,128)S(1)} %get-tuple-element.170), channel_id=1, source_target_pairs={{0,10},{1,11},{2,12},{3,13},{4,14},{5,15},{6,16},{7,17},{8,18},{9,... | collective-permute-start | bytes 442376
  902.5 52.9 %collective-permute-start.10 = (f32[16,2304]{1,0:T(8,128)S(1)}, f32[16,2304]{1,0:T(8,128)}, u32[]{:S(2)}, u32[]{:S(2)}) collective-permute-start(f32[16,2304]{1,0:T(8,128)S(1)} %get-tuple-element.170), channel_id=1, source_target_pairs={{0,9},{1,10},{2,11},{3,12},{4,13},{5,14},{6,15},{7,16},{8,17},{9,1... | collective-permute-start | bytes 442376
  904.5 53.2 %collective-permute-start.9 = (f32[16,2304]{1,0:T(8,128)S(1)}, f32[16,2304]{1,0:T(8,128)}, u32[]{:S(2)}, u32[]{:S(2)}) collective-permute-start(f32[16,2304]{1,0:T(8,128)S(1)} %get-tuple-element.170), channel_id=1, source_target_pairs={{0,8},{1,9},{2,10},{3,11},{4,12},{5,13},{6,14},{7,15},{8,16},{9,17... | collective-permute-start | bytes 442376
  910.3 49.9 %collective-permute-start.8 = (f32[16,2304]{1,0:T(8,128)S(1)}, f32[16,2304]{1,0:T(8,128)}, u32[]{:S(2)}, u32[]{:S(2)}) collective-permute-start(f32[16,2304]{1,0:T(8,128)S(1)} %get-tuple-element.170), channel_id=1, source_target_pairs={{0,7},{1,8},{2,9},{3,10},{4,11},{5,12},{6,13},{7,14},{8,15},{9,16}... | collective-permute-start | bytes 442376
  912.6 53.9 %collective-permute-start.7 = (f32[16,2304]{1,0:T(8,128)S(1)}, f32[16,2304]{1,0:T(8,128)}, u32[]{:S(2)}, u32[]{:S(2)}) collective-permute-start(f32[16,2304]{1,0:T(8,128)S(1)} %get-tuple-element.170), channel_id=1, source_target_pairs={{0,6},{1,7},{2,8},{3,9},{4,10},{5,11},{6,12},{7,13},{8,14},{9,15},... | collective-permute-start | bytes 442376
  945.5 23.7 %collective-permute-start.6 = (f32[16,2304]{1,0:T(8,128)S(1)}, f32[16,2304]{1,0:T(8,128)S(1)}, u32[]{:S(2)}, u32[]{:S(2)}) collective-permute-start(f32[16,2304]{1,0:T(8,128)S(1)} %get-tuple-element.170), channel_id=1, source_target_pairs={{0,5},{1,6},{2,7},{3,8},{4,9},{5,10},{6,11},{7,12},{8,13},{9,14},{... | collective-permute-start | bytes 442376
  955.5 13.7 %collective-permute-start.5 = (f32[16,2304]{1,0:T(8,128)S(1)}, f32[16,2304]{1,0:T(8,128)S(1)}, u32[]{:S(2)}, u32[]{:S(2)}) collective-permute-start(f32[16,2304]{1,0:T(8,128)S(1)} %get-tuple-element.170), channel_id=1, source_target_pairs={{0,4},{1,5},{2,6},{3,7},{4,8},{5,9},{6,10},{7,11},{8,12},{9,13},{1... | collective-permute-start | bytes 442376
  957.7 14.3 %collective-permute-start.4 = (f32[16,2304]{1,0:T(8,128)S(1)}, f32[16,2304]{1,0:T(8,128)S(1)}, u32[]{:S(2)}, u32[]{:S(2)}) collective-permute-start(f32[16,2304]{1,0:T(8,128)S(1)} %get-tuple-element.170), channel_id=1, source_target_pairs={{0,3},{1,4},{2,5},{3,6},{4,7},{5,8},{6,9},{7,10},{8,11},{9,12},{10... | collective-permute-start | bytes 442376
  (100 other events, 2408.9 us)
Sparse Core Ops, SparseCore 0:
  20.6 101.9 all-gather.1
